TPU v7x, 128 devices: a whole 4x4x4 slice. The times are simulated.
128 devices in a mesh: tm: 4 (over y), clus: 32 (over z, x, core).
Axes of the slice: x: 4, y: 4, z: 4, core: 2. Of those that a mesh axis runs over, the one named last changes fastest.
Arguments:
- embedding: bfloat16 [131072, 384], P(('tm', 'clus')), may hold values from -6 to 6
- cluster_of: int32 [131072], P(('tm', 'clus')), may hold values from 0 to 255, as said below
Outputs:
- mixed: bfloat16 [131072, 384], P(('tm', 'clus'))
Inputs may be any that keep to these rules, and one draw needn't show every extreme that they name: `cluster_of`: of the 1024 invoices of one device at most 16 belong to the two clusters of one owner, and on every device some owner receives exactly 16; each cluster holds at most 1024 invoices, and in every draw both clusters of some owner hold exactly 1024.
All inputs are finite; a program needn't handle non-finite values.
Results may differ from a plain program's by a relative error of at most 0.0035.
Values may be sent and summed in bfloat16 or wider, within the bound.
A program may use at most 64 MiB of HBM per device.

v0:
```python
import jax
import jax.numpy as jnp
from jax import lax
from jax.sharding import PartitionSpec as P

TAU = 40.0


def unit_rows(rows):
    values = rows.astype(jnp.float32)
    return (values * lax.rsqrt(jnp.sum(values * values, axis=1, keepdims=True) + 1e-06)).astype(
        jnp.bfloat16
    )


def cluster_result(rows, units, present):
    capacity, width = rows.shape
    block = capacity // 4
    totals = [jnp.zeros((block, width), jnp.float32) for index in range(4)]
    masses = [jnp.zeros((block,), jnp.float32) for index in range(4)]
    inner = jnp.arange(block, dtype=jnp.int32)
    for left in range(4):
        for right in range(left, 4):
            units_left = units[left * block : (left + 1) * block]
            units_right = units[right * block : (right + 1) * block]
            rows_left = rows[left * block : (left + 1) * block]
            rows_right = rows[right * block : (right + 1) * block]
            keep = (
                present[left * block : (left + 1) * block][:, None]
                & present[right * block : (right + 1) * block][None, :]
            )
            if left == right:
                keep = keep & (inner[:, None] != inner[None, :])

            def scored(
                unused,
                units_left=units_left,
                units_right=units_right,
                rows_left=rows_left,
                rows_right=rows_right,
                keep=keep,
                diagonal=left == right,
            ):
                scores = jnp.dot(units_left, units_right.T, preferred_element_type=jnp.float32)
                weight = jnp.where(keep, jnp.exp(TAU * scores), jnp.zeros((), jnp.float32)).astype(
                    jnp.bfloat16
                )
                wide = weight.astype(jnp.float32)
                total_left = jnp.dot(weight, rows_right, preferred_element_type=jnp.float32)
                mass_left = jnp.sum(wide, axis=1)
                if diagonal:
                    return (
                        total_left,
                        mass_left,
                        jnp.zeros_like(total_left),
                        jnp.zeros_like(mass_left),
                    )
                total_right = lax.dot_general(
                    weight, rows_left, (((0,), (0,)), ((), ())), preferred_element_type=jnp.float32
                )
                return (total_left, mass_left, total_right, jnp.sum(wide, axis=0))

            parts = scored(None)
            totals[left] = totals[left] + parts[0]
            masses[left] = masses[left] + parts[1]
            if left != right:
                totals[right] = totals[right] + parts[2]
                masses[right] = masses[right] + parts[3]
    total = jnp.concatenate(totals, axis=0)
    mass = jnp.concatenate(masses, axis=0)
    return (rows.astype(jnp.float32) - total / (1.0 + mass)[:, None]).astype(jnp.bfloat16)


def on_device(embedding, cluster_of):
    rows_here, width = embedding.shape
    time_count = lax.axis_size("tm")
    owner_count = lax.axis_size("clus")
    owners = time_count * owner_count
    slot = 2 * rows_here // owners
    owner = cluster_of // 2
    hits = (owner[:, None] == jnp.arange(owners, dtype=jnp.int32)[None, :]).astype(jnp.int32)
    rank = jnp.sum(jnp.cumsum(hits, axis=0) * hits, axis=1) - 1
    target = owner * slot + rank
    outgoing = jnp.zeros((owners * slot, width), jnp.bfloat16).at[target].set(embedding)
    labels = jnp.full((owners * slot,), -1, jnp.int32).at[target].set(cluster_of)
    arrived, arrived_labels = (
        lax.all_to_all(
            outgoing.reshape(owners, slot, width),
            ("tm", "clus"),
            split_axis=0,
            concat_axis=0,
            tiled=True,
        ),
        lax.all_to_all(
            labels.reshape(owners, slot), ("tm", "clus"), split_axis=0, concat_axis=0, tiled=True
        ),
    )
    arrived = arrived.reshape(owners * slot, width)
    arrived_labels = arrived_labels.reshape(owners * slot)
    present = arrived_labels >= 0
    local = arrived_labels % 2
    member = (
        (local[:, None] == jnp.arange(2, dtype=jnp.int32)[None, :]) & present[:, None]
    ).astype(jnp.int32)
    place = jnp.sum(jnp.cumsum(member, axis=0) * member, axis=1) - 1
    position = jnp.where(present, local * rows_here + place, 2 * rows_here)
    grouped = jnp.zeros((2 * rows_here, width), jnp.bfloat16).at[position].set(arrived, mode="drop")
    filled = jnp.zeros((2 * rows_here,), jnp.bool_).at[position].set(True, mode="drop")
    units = unit_rows(grouped)
    results = []
    for cluster in range(2):
        rows_cluster = grouped[cluster * rows_here : (cluster + 1) * rows_here]
        units_cluster = units[cluster * rows_here : (cluster + 1) * rows_here]
        filled_cluster = filled[cluster * rows_here : (cluster + 1) * rows_here]
        results.append(cluster_result(rows_cluster, units_cluster, filled_cluster))
    merged = jnp.concatenate(results, axis=0)
    answers = jnp.take(merged, position, axis=0, mode="fill", fill_value=0)
    returned = lax.all_to_all(
        answers.reshape(owners, slot, width),
        ("tm", "clus"),
        split_axis=0,
        concat_axis=0,
        tiled=True,
    )
    returned = returned.reshape(owners * slot, width)
    return returned[target]


def solution(mesh):
    return jax.shard_map(
        on_device,
        mesh=mesh,
        in_specs=(P(("tm", "clus"), None), P(("tm", "clus"))),
        out_specs=P(("tm", "clus"), None),
        check_vma=False,
    )
```

profile of v0, /device:TPU:1, one launch (start us, length us, event | category | flops | bytes accessed | tf_op | source)
XLA Modules:
  0.0 128.3 jit_solution(12756565551991006060)
XLA Ops:
  0.0 0.7 add_select_fusion.3
  1.2 0.4 fusion.70
  1.6 4.3 %scatter_custom_fusion = s32[2048]{0:T(1024)S(1)} fusion(s32[1024]{0:T(1024)S(1)} %get-tuple-element.30, s32[1024]{0:T(1024)S(1)} %copy-done, s32[]{:T(128)} %constant.64.clone.1), kind=kCustom, calls=%fused_computation.295 | custom fusion | bytes 8196 | tf_op jit(solution)/shard_map/scatter | solution.py:85
  5.9 0.7 all_to_all.12
  6.6 11.5 %all-to-all-start = ((s32[128,1,16]{2,1,0:T(1,128)}), s32[128,1,16]{2,1,0:T(1,128)S(1)}, u32[]{:S(2)}, u32[]{:S(2)}) async-start(s32[128,1,16]{2,1,0:T(1,128)} %bitcast.4), calls=%async_computation | async-start | bytes 131072 | tf_op jit(solution)/shard_map/all_to_all | solution.py:94
  18.1 6.8 %scatter_custom_fusion.1 = bf16[2048,384]{1,0:T(8,128)(2,1)} fusion(s32[1024]{0:T(1024)S(1)} %get-tuple-element.30, bf16[1024,384]{1,0:T(8,128)(2,1)} %param.2, bf16[]{:T(256)} %constant.72.clone.1), kind=kCustom, calls=%fused_computation.124 | custom fusion | bytes 1573376 | tf_op jit(solution)/shard_map/scatter | solution.py:84
  24.9 2.6 %all-to-all-done = s32[128,1,16]{2,1,0:T(1,128)S(1)} async-done(((s32[128,1,16]{2,1,0:T(1,128)}), s32[128,1,16]{2,1,0:T(1,128)S(1)}, u32[]{:S(2)}, u32[]{:S(2)}) %all-to-all-start) | async-done | bytes 8224 | tf_op jit(solution)/shard_map/all_to_all | solution.py:94
  27.6 7.1 %all-to-all-start.1 = ((bf16[128,16,384]{2,1,0:T(8,128)(2,1)}), bf16[128,16,384]{2,1,0:T(8,128)(2,1)S(1)}, u32[]{:S(2)}, u32[]{:S(2)}) async-start(bf16[128,16,384]{2,1,0:T(8,128)(2,1)} %bitcast.9), calls=%async_computation.1 | async-start | bytes 3145728 | tf_op jit(solution)/shard_map/all_to_all | solution.py:87
  34.8 0.6 reduce-window.16
  35.9 0.5 broadcast.330
  36.4 0.8 reduce.9
  37.6 9.3 %scatter_custom_fusion.3 = pred[2048]{0:T(1024)(128)(4,1)S(1)} fusion(s32[2048]{0:T(1024)S(1)} %bitcast.73, pred[2048]{0:T(1024)(128)(4,1)S(1)} %broadcast.263, pred[]{:T(512)} %constant.73.clone.1), kind=kCustom, calls=%fused_computation.298 | custom fusion | bytes 2049 | tf_op jit(solution)/shard_map/scatter | solution.py:108
  47.0 12.6 %all-to-all-done.1 = bf16[128,16,384]{2,1,0:T(8,128)(2,1)S(1)} async-done(((bf16[128,16,384]{2,1,0:T(8,128)(2,1)}), bf16[128,16,384]{2,1,0:T(8,128)(2,1)S(1)}, u32[]{:S(2)}, u32[]{:S(2)}) %all-to-all-start.1) | async-done | bytes 1572896 | tf_op jit(solution)/shard_map/all_to_all | solution.py:87
  59.6 9.9 %scatter_custom_fusion.2 = bf16[2048,384]{1,0:T(8,128)(2,1)S(1)} fusion(s32[2048]{0:T(1024)S(1)} %bitcast.75, bf16[2048,384]{1,0:T(8,128)(2,1)S(1)} %bitcast.71, bf16[]{:T(256)} %constant.72.clone.1), kind=kCustom, calls=%fused_computation.122 | custom fusion | bytes 1572866 | tf_op jit(solution)/shard_map/scatter | solution.py:107
  69.5 0.4 fusion
  69.9 0.3 fusion.1
  70.3 0.3 convert_reduce_fusion.30
  70.6 0.3 convert_reduce_fusion.29
  70.9 0.4 convert_reduce_fusion.17
  71.2 0.3 convert_reduce_fusion.28
  71.5 0.4 convert_reduce_fusion.15
  71.9 0.3 convert_reduce_fusion.31
  72.1 0.4 convert_reduce_fusion.23
  72.5 0.4 convert_reduce_fusion.13
  72.8 0.4 convert_reduce_fusion.19
  73.2 0.4 convert_reduce_fusion.21
  73.6 0.3 convert_reduce_fusion.26
  73.8 0.3 convert_reduce_fusion.25
  74.1 0.4 convert_reduce_fusion.5
  74.5 0.3 convert_reduce_fusion.24
  74.8 0.4 convert_reduce_fusion.3
  75.1 0.3 convert_reduce_fusion.27
  75.4 0.4 convert_reduce_fusion.11
  75.8 0.4 convert_reduce_fusion.1
  76.1 0.4 convert_reduce_fusion.7
  76.5 0.4 convert_reduce_fusion.9
  78.0 0.3 convolution_add_fusion.10
  80.0 0.3 convolution_add_fusion.7
  80.3 0.3 convolution_add_fusion.6
  81.5 0.3 convolution_add_fusion.22
  82.0 0.3 convolution_add_fusion.21
  83.5 0.3 convolution_add_fusion.20
  84.2 0.3 convolution_add_fusion
  84.9 1.4 %fusion.3 = (bf16[1024,384]{1,0:T(8,128)(2,1)S(1)}, bf16[1024,384]{1,0:T(8,128)(2,1)S(1)}) fusion(f32[256,384]{1,0:T(8,128)S(1)} %convolution_add_fusion.12, f32[256,384]{1,0:T(8,128)S(1)} %convolution_add_fusion.15, f32[256,384]{1,0:T(8,128)S(1)} %convolution_add_fusion.18, f32[256,384]{1,0:T(8,128)S(1)} %convolution_add_fusion.21, ...), kind=kLoop, calls=%fused_computation.12 | loop fusion | flops 5505024 | bytes 6299648 | tf_op jit(solution)/shard_map/convert_element_type | solution.py:71
  86.5 7.5 %gather_fusion = bf16[2048,384]{1,0:T(8,128)(2,1)S(1)} fusion(bf16[2048,384]{1,0:T(8,128)(2,1)S(1)} %pad_maximum_fusion, s32[2048]{0:T(1024)S(1)} %broadcast_clamp_fusion), kind=kCustom, calls=%fused_computation | custom fusion | bytes 3153920 | tf_op jit(solution)/shard_map/jit(_take)/gather | solution.py:117
  93.9 0.5 broadcast_select_fusion
  94.4 29.0 %all_to_all.19 = bf16[128,16,384]{2,1,0:T(8,128)(2,1)S(1)} all-to-all(bf16[128,16,384]{2,1,0:T(8,128)(2,1)S(1)} %broadcast_select_fusion), channel_id=1, replica_groups=mesh['tm'=4,'clus'=32] {'tm','clus'}, dimensions={0} | all-to-all | bytes 3145728 | tf_op jit(solution)/shard_map/all_to_all | solution.py:118
  123.3 5.0 %gather_fusion.1 = bf16[1024,384]{1,0:T(8,128)(2,1)} fusion(bf16[2048,384]{1,0:T(8,128)(2,1)S(1)} %bitcast.66, s32[1024]{0:T(1024)S(1)} %get-tuple-element.29), kind=kCustom, calls=%fused_computation.1 | custom fusion | bytes 1576960 | tf_op jit(solution)/shard_map/gather | solution.py:126
  (62 shorter events, 7.6 us)
Async XLA Ops:
  0.8 0.8 copy-start
  6.6 20.9 %all-to-all-start = ((s32[128,1,16]{2,1,0:T(1,128)}), s32[128,1,16]{2,1,0:T(1,128)S(1)}, u32[]{:S(2)}, u32[]{:S(2)}) async-start(s32[128,1,16]{2,1,0:T(1,128)} %bitcast.4), calls=%async_computation | async-start | bytes 131072 | tf_op jit(solution)/shard_map/all_to_all | solution.py:94
  27.6 32.1 %all-to-all-start.1 = ((bf16[128,16,384]{2,1,0:T(8,128)(2,1)}), bf16[128,16,384]{2,1,0:T(8,128)(2,1)S(1)}, u32[]{:S(2)}, u32[]{:S(2)}) async-start(bf16[128,16,384]{2,1,0:T(8,128)(2,1)} %bitcast.9), calls=%async_computation.1 | async-start | bytes 3145728 | tf_op jit(solution)/shard_map/all_to_all | solution.py:87
where the time goes:
time: 129 us; the launch traced here: 128 us
  local copies, waits for them, and re-layouts  44.7 us (35%)
  blocking collectives  29 us (22%)
  starting transfers between devices  18.6 us (14%)
  waiting for transfers between devices  15.3 us (12%)
  matrix products  14.2 us (11%)
  other arithmetic  6.03 us (5%)
    all_to_all x1, blocking collectives, on_device(): lax.all_to_all(answers.reshape(owners, slot, width), ('tm', 'clus'), spli...  29 us
    all_to_all x1, waiting for transfers between devices, on_device(): lax.all_to_all(outgoing.reshape(owners, slot, width), ('tm', 'clus'), spl...  12.6 us
    all_to_all x1, starting transfers between devices, on_device(): lax.all_to_all(labels.reshape(owners, slot), ('tm', 'clus'), split_axis=0...  11.5 us
    scatter x1, local copies, waits for them, and re-layouts, on_device(): jnp.zeros((2 * rows_here, width), jnp.bfloat16).at[position]  9.9 us
    scatter x1, local copies, waits for them, and re-layouts, on_device(): jnp.zeros((2 * rows_here,), jnp.bool_).at[position].set(True, mode='drop')  9.29 us
    gather x1, local copies, waits for them, and re-layouts, on_device(): answers = jnp.take(merged, position, axis=0, mode='fill', fill_value=0)  7.46 us
    all_to_all x1, starting transfers between devices, on_device(): lax.all_to_all(outgoing.reshape(owners, slot, width), ('tm', 'clus'), spl...  7.14 us
    scatter x1, local copies, waits for them, and re-layouts, on_device(): jnp.zeros((owners * slot, width), jnp.bfloat16).at[target].set(embedding)  6.8 us
  transfers between devices with their start and end apart: 2, of which 2 were waited for; matrix products, arithmetic and copies ran while one was open for 15% of the time, Pallas kernels for 0%

commit v1 on v0

v1 whole, which is shorter than its diff:
```python
import functools
import math

import jax
import jax.numpy as jnp
from jax import lax
from jax.experimental import pallas as pl
from jax.experimental.pallas import tpu as pltpu
from jax.sharding import PartitionSpec as P

MESH = pl.DeviceIdType.MESH
BF16, F32, I32 = jnp.bfloat16, jnp.float32, jnp.int32
N = 128
ROWS = 1024
E = 384
SLOT = 16
SLOTS = N * SLOT
CH = 256
NCH = SLOTS // CH
PER = CH // SLOT
STEP, BACK = 37, 45
SCALE = 40.0 * math.log2(math.e)
APART = 16.0


def rank_of(shift):
    return (shift * BACK) & (N - 1)


def coords():
    tm, cl = lax.axis_index("tm"), lax.axis_index("clus")
    return tm, cl // 8, (cl // 2) % 4, cl % 2


def partner(k, sign):
    shift = (k * STEP) % N
    y, z, x, c = coords()
    y = (y + 4 + sign * (shift // 32)) % 4
    z = (z + 4 + sign * ((shift // 8) % 4)) % 4
    x = (x + 4 + sign * ((shift // 2) % 4)) % 4
    c = (c + shift) % 2
    return (y, z * 8 + x * 2 + c)


def at(start, size):
    return pl.ds(pl.multiple_of(start, 16), size)


def kernel(
    emb, labels, out,
    send, meta_send, recv, meta_recv, rows, left, right, total, result, returned, pick,
    send_sem, meta_send_sem, back_sem, recv_sem, meta_sem, return_sem,
):
    barrier = pltpu.get_barrier_semaphore()

    def greet(k, carry):
        pl.semaphore_signal(barrier, inc=1, device_id=partner(k, 1), device_id_type=MESH)
        return carry

    lax.fori_loop(1, N, greet, 0)

    y, z, x, c = coords()
    label = labels[...]
    owner = label >> 1
    dy, dz = ((owner >> 5) - y) & 3, ((owner >> 3) - z) & 3
    dx, dc = ((owner >> 1) - x) & 3, (owner - c) & 1
    order = rank_of(dy * 32 + dz * 8 + dx * 2 + dc)
    hits = (order == lax.broadcasted_iota(I32, (N, ROWS), 0)).astype(F32)
    upper = (
        lax.broadcasted_iota(I32, (CH, CH), 0) <= lax.broadcasted_iota(I32, (CH, CH), 1)
    ).astype(BF16)
    before = jnp.zeros((N, 1), F32)
    ranks = []
    for part in range(ROWS // CH):
        hit = hits[:, part * CH : (part + 1) * CH]
        count = jnp.dot(hit.astype(BF16), upper, preferred_element_type=F32) + before
        ranks.append(jnp.sum(count * hit, axis=0, keepdims=True))
        before = before + jnp.sum(hit, axis=1, keepdims=True)
    rank = jnp.concatenate(ranks, axis=1).astype(I32) - 1
    target = order * SLOT + rank

    lane_of = lax.broadcasted_iota(I32, (N, ROWS), 0)
    value = jnp.where(lane_of == rank, (label & 1) + 1, 0).astype(BF16)
    meta = lax.dot_general(
        hits.astype(BF16), value, (((1,), (1,)), ((), ())), preferred_element_type=F32
    )
    meta_send[...] = meta.astype(I32).reshape(N, 1, N)

    pl.semaphore_wait(barrier, N - 1)

    def send_one(k, carry):
        device = partner(k, 1)
        chunk = k // PER
        pltpu.make_async_remote_copy(
            src_ref=meta_send.at[k], dst_ref=meta_recv.at[k],
            send_sem=meta_send_sem, recv_sem=meta_sem.at[chunk],
            device_id=device, device_id_type=MESH,
        ).start()
        pltpu.make_async_remote_copy(
            src_ref=send.at[at(k * SLOT, SLOT)], dst_ref=recv.at[at(k * SLOT, SLOT)],
            send_sem=send_sem, recv_sem=recv_sem.at[chunk],
            device_id=device, device_id_type=MESH,
        ).start()
        return carry

    def pack(chunk, carry):
        slot = lax.broadcasted_iota(I32, (CH, ROWS), 0) + chunk * CH
        chosen = (slot == target).astype(BF16)
        packed = jnp.dot(chosen, emb[...], preferred_element_type=F32)
        send[at(chunk * CH, CH), :] = packed.astype(BF16)
        lax.fori_loop(jnp.maximum(chunk * PER, 1), (chunk + 1) * PER, send_one, 0)
        return carry

    lax.fori_loop(0, NCH, pack, 0)

    column = jnp.broadcast_to(target, (N, ROWS)).T
    lanes = lax.broadcasted_iota(I32, (ROWS, N), 1)
    for part in range(SLOTS // N):
        pick[:, part * N : (part + 1) * N] = (column == lanes + part * N).astype(BF16)

    rows[:, E:] = jnp.ones((SLOTS, N), BF16)
    diagonal = lax.broadcasted_iota(I32, (CH, CH), 0) == lax.broadcasted_iota(I32, (CH, CH), 1)
    lane = lax.broadcasted_iota(I32, (CH, N), 1)
    own_slot = lax.broadcasted_iota(I32, (PER, SLOT, N), 1) == lax.broadcasted_iota(
        I32, (PER, SLOT, N), 2
    )
    spread = jnp.ones((N, N), BF16)

    def weights(a, b):
        score = lax.dot_general(
            left[at(a * CH, CH), :], right[at(b * CH, CH), :],
            (((1,), (1,)), ((), ())), preferred_element_type=F32,
        )
        return jnp.exp2(score * SCALE)

    for chunk in range(NCH):
        first = 1 if chunk == 0 else 0
        base, count = chunk * CH + first * SLOT, CH - first * SLOT
        here = slice(chunk * CH, (chunk + 1) * CH)
        pltpu.make_async_copy(
            meta_recv.at[chunk * PER + first : (chunk + 1) * PER],
            meta_recv.at[chunk * PER + first : (chunk + 1) * PER],
            meta_sem.at[chunk],
        ).wait()
        pltpu.make_async_copy(
            recv.at[base : base + count], recv.at[base : base + count], recv_sem.at[chunk]
        ).wait()
        if chunk == 0:
            recv[0:SLOT, :] = send[0:SLOT, :]
            meta_recv[0] = meta_send[0]
        marks = meta_recv[chunk * PER : (chunk + 1) * PER].reshape(PER, 1, N)
        marks = jnp.where(own_slot, jnp.broadcast_to(marks, (PER, SLOT, N)), 0)
        marks = marks.astype(F32).reshape(CH, N).astype(BF16)
        kind = jnp.dot(marks, spread, preferred_element_type=F32).astype(I32)
        kind = jnp.where(kind == 0, 2, kind - 1)
        values = recv[here, :]
        wide = values.astype(F32)
        unit = wide * lax.rsqrt(jnp.sum(wide * wide, axis=1, keepdims=True) + 1e-06)
        unit = unit.astype(BF16)
        rows[here, :E] = values
        left[here, :E] = unit
        right[here, :E] = unit
        left[here, E:] = ((lane < 3) & (lane != kind)).astype(BF16)
        right[here, E:] = jnp.where(lane == kind, -APART, 0.0).astype(BF16)

        own = jnp.where(diagonal, 0.0, weights(chunk, chunk)).astype(BF16)
        total[here, :] = jnp.dot(own, rows[here, :], preferred_element_type=F32)

        def earlier(b, carry, chunk=chunk, here=here):
            there = at(b * CH, CH)
            weight = weights(chunk, b).astype(BF16)
            total[here, :] += jnp.dot(weight, rows[there, :], preferred_element_type=F32)
            return carry

        lax.fori_loop(0, chunk, earlier, 0)

        def later(b, carry, chunk=chunk, here=here):
            there = at(b * CH, CH)
            weight = weights(b, chunk).astype(BF16)
            total[there, :] += jnp.dot(weight, rows[here, :], preferred_element_type=F32)
            return carry

        if chunk < NCH - 1:
            lax.fori_loop(0, chunk, later, 0)

    def return_one(k, carry):
        pltpu.make_async_remote_copy(
            src_ref=result.at[at(k * SLOT, SLOT)], dst_ref=returned.at[at(k * SLOT, SLOT)],
            send_sem=back_sem, recv_sem=return_sem.at[k // PER],
            device_id=partner(k, -1), device_id_type=MESH,
        ).start()
        return carry

    def finish(b, carry):
        there = at(b * CH, CH)
        full = total[there, :]

        def last(full):
            weight = weights(b, NCH - 1).astype(BF16)
            return full + jnp.dot(
                weight, rows[(NCH - 1) * CH :, :], preferred_element_type=F32
            )

        full = lax.cond(b < NCH - 1, last, lambda full: full, full)
        inverse = 1.0 / (1.0 + full[:, E:])
        for part in range(E // N):
            span = slice(part * N, (part + 1) * N)
            mixed = recv[there, span].astype(F32) - full[:, span] * inverse
            result[there, span] = mixed.astype(BF16)
        lax.fori_loop(jnp.maximum(b * PER, 1), (b + 1) * PER, return_one, 0)
        return carry

    lax.fori_loop(0, NCH, finish, 0)
    returned[0:SLOT, :] = result[0:SLOT, :]

    for chunk in range(NCH):
        first = 1 if chunk == 0 else 0
        base, count = chunk * CH + first * SLOT, CH - first * SLOT
        here = slice(chunk * CH, (chunk + 1) * CH)
        pltpu.make_async_copy(
            returned.at[base : base + count], returned.at[base : base + count],
            return_sem.at[chunk],
        ).wait()
        part = jnp.dot(pick[:, here], returned[here, :], preferred_element_type=F32).astype(BF16)
        if chunk == 0:
            out[...] = part
        else:
            out[...] += part

    sent = slice(SLOT, SLOTS)
    pltpu.make_async_copy(send.at[sent], send.at[sent], send_sem).wait()
    pltpu.make_async_copy(meta_send.at[1:N], meta_send.at[1:N], meta_send_sem).wait()
    pltpu.make_async_copy(result.at[sent], result.at[sent], back_sem).wait()


def on_device(embedding, cluster_of):
    return pl.pallas_call(
        kernel,
        out_shape=jax.ShapeDtypeStruct((ROWS, E), BF16),
        in_specs=[pl.BlockSpec(memory_space=pltpu.VMEM)] * 2,
        out_specs=pl.BlockSpec(memory_space=pltpu.VMEM),
        scratch_shapes=[
            pltpu.VMEM((SLOTS, E), BF16),
            pltpu.VMEM((N, 1, N), I32),
            pltpu.VMEM((SLOTS, E), BF16),
            pltpu.VMEM((N, 1, N), I32),
            pltpu.VMEM((SLOTS, E + N), BF16),
            pltpu.VMEM((SLOTS, E + N), BF16),
            pltpu.VMEM((SLOTS, E + N), BF16),
            pltpu.VMEM((SLOTS, E + N), F32),
            pltpu.VMEM((SLOTS, E), BF16),
            pltpu.VMEM((SLOTS, E), BF16),
            pltpu.VMEM((ROWS, SLOTS), BF16),
            pltpu.SemaphoreType.DMA,
            pltpu.SemaphoreType.DMA,
            pltpu.SemaphoreType.DMA,
            pltpu.SemaphoreType.DMA((NCH,)),
            pltpu.SemaphoreType.DMA((NCH,)),
            pltpu.SemaphoreType.DMA((NCH,)),
        ],
        compiler_params=pltpu.CompilerParams(
            collective_id=0, has_side_effects=True, vmem_limit_bytes=56 << 20
        ),
    )(embedding, cluster_of.reshape(1, ROWS))


def solution(mesh):
    return jax.shard_map(
        on_device,
        mesh=mesh,
        in_specs=(P(("tm", "clus"), None), P(("tm", "clus"))),
        out_specs=P(("tm", "clus"), None),
        check_vma=False,
    )
```

time: 129 us -> 82.9 us (0.64)
  Pallas kernels: 0 us -> 80.6 us
  local copies, waits for them, and re-layouts: 44.7 us -> 2.09 us
  blocking collectives: 29 us -> 0 us
  starting transfers between devices: 18.6 us -> 0 us
  waiting for transfers between devices: 15.3 us -> 0 us
  matrix products: 14.2 us -> 0 us
  other arithmetic: 6.03 us -> 0 us
    pallas_call x0 -> x1, Pallas kernels: none -> 80.6 us  [on_device(): pl.pallas_call(kernel, out_shape=jax.ShapeDtypeStruct((ROWS, E), BF16), i...]
    scatter x4 -> x0, local copies, waits for them, and re-layouts: 30.3 us -> none  [the longest x1 9.9 us: on_device(): jnp.zeros((2 * rows_here, width), jnp.bfloat16).at[position]]
    all_to_all x1 -> x0, blocking collectives: 29 us -> none  [on_device(): lax.all_to_all(answers.reshape(owners, slot, width), ('tm', 'clus'), spli...]
    all_to_all x2 -> x0, starting transfers between devices: 18.6 us -> none  [the longest x1 11.5 us: on_device(): lax.all_to_all(labels.reshape(owners, slot), ('tm', 'clus'), split_axis=0...]
    all_to_all x2 -> x0, waiting for transfers between devices: 15.3 us -> none  [the longest x1 12.6 us: on_device(): lax.all_to_all(outgoing.reshape(owners, slot, width), ('tm', 'clus'), spl...]
    dot_general x52 -> x0, matrix products: 14.2 us -> none  [the longest x20 6.51 us: scored(): jnp.dot(units_left, units_right.T, preferred_element_type=jnp.float32)]
    gather x2 -> x0, local copies, waits for them, and re-layouts: 12.5 us -> none  [the longest x1 7.46 us: on_device(): answers = jnp.take(merged, position, axis=0, mode='fill', fill_value=0)]
    unnamed x2 -> x1, local copies, waits for them, and re-layouts: 0.01 us -> 2.09 us
  transfers between devices with their start and end apart: 2 -> 0, of which waited for: 2 -> 0; matrix products, arithmetic and copies ran while one was open for 15% -> 0% of each run, Pallas kernels for 0% -> 0%
where the time goes in v1:
time: 82.9 us; the launch traced here: 82.7 us
  Pallas kernels  80.6 us (97%)
  local copies, waits for them, and re-layouts  2.09 us (3%)
    pallas_call x1, Pallas kernels, on_device(): pl.pallas_call(kernel, out_shape=jax.ShapeDtypeStruct((ROWS, E), BF16), i...  80.6 us
    unnamed x1, local copies, waits for them, and re-layouts  2.09 us

profile of v1, /device:TPU:1, one launch (start us, length us, event | category | flops | bytes accessed | tf_op | source)
XLA Modules:
  0.0 82.7 jit_solution(8864221037435251065)
XLA Ops:
  0.0 80.6 %shard_map.28 = bf16[1024,384]{1,0:T(8,128)(2,1)} custom-call(bf16[1024,384]{1,0:T(8,128)(2,1)} %emb.1, s32[1,1024]{1,0:T(1,128)} %bitcast.1), custom_call_target="tpu_custom_call" | custom-call | tf_op jit(solution)/shard_map/pallas_call | solution.py:237
  80.6 2.1 %copy.4 = bf16[1024,384]{1,0:T(8,128)(2,1)} copy(bf16[1024,384]{1,0:T(8,128)(2,1)} %shard_map.28) | data formatting | bytes 1572864

commit v2 on v1

--- a/solution.py
+++ b/solution.py
@@ -1,6 +1,3 @@
-import functools
-import math
-
 import jax
 import jax.numpy as jnp
 from jax import lax
@@ -18,8 +15,7 @@
 CH = 256
 NCH = SLOTS // CH
 PER = CH // SLOT
-STEP, BACK = 37, 45
-SCALE = 40.0 * math.log2(math.e)
+STEP, BACK = 91, 83
 APART = 16.0
 
 
@@ -33,12 +29,12 @@
 
 
 def partner(k, sign):
-    shift = (k * STEP) % N
+    shift = lax.rem(k * STEP, N)
+    dy, dz, dx = lax.div(shift, 32), lax.rem(lax.div(shift, 8), 4), lax.rem(lax.div(shift, 2), 4)
     y, z, x, c = coords()
-    y = (y + 4 + sign * (shift // 32)) % 4
-    z = (z + 4 + sign * ((shift // 8) % 4)) % 4
-    x = (x + 4 + sign * ((shift // 2) % 4)) % 4
-    c = (c + shift) % 2
+    if sign < 0:
+        dy, dz, dx = 4 - dy, 4 - dz, 4 - dx
+    y, z, x, c = lax.rem(y + dy, 4), lax.rem(z + dz, 4), lax.rem(x + dx, 4), lax.rem(c + shift, 2)
     return (y, z * 8 + x * 2 + c)
 
 
@@ -47,19 +43,28 @@
 
 
 def kernel(
-    emb, labels, out,
-    send, meta_send, recv, meta_recv, rows, left, right, total, result, returned, pick,
-    send_sem, meta_send_sem, back_sem, recv_sem, meta_sem, return_sem,
+    emb_hbm, labels, out,
+    emb, send, meta_send, recv, meta_recv, rows, left, right, total, result, returned, pick,
+    fetch_sem, planes_sem, send_sem, meta_send_sem, back_sem, recv_sem, meta_sem, return_sem,
 ):
+    fetch = pltpu.make_async_copy(emb_hbm, emb, fetch_sem)
+    fetch.start()
+
+    y, z, x, c = coords()
     barrier = pltpu.get_barrier_semaphore()
-
-    def greet(k, carry):
-        pl.semaphore_signal(barrier, inc=1, device_id=partner(k, 1), device_id_type=MESH)
-        return carry
-
-    lax.fori_loop(1, N, greet, 0)
-
-    y, z, x, c = coords()
+    plane = [(a, b) for a in range(4) for b in range(4) if (a, b) != (0, 0)]
+    line = [(a, b) for a in range(4) for b in range(2) if (a, b) != (0, 0)]
+    ys, zs = [lax.rem(y + d, 4) for d in range(4)], [lax.rem(z + d, 4) * 8 for d in range(4)]
+    xs, cs = [lax.rem(x + d, 4) * 2 for d in range(4)], [c, 1 - c]
+    for a, b in plane:
+        pl.semaphore_signal(
+            barrier, inc=1, device_id=(ys[a], zs[b] + (xs[0] + c)), device_id_type=MESH
+        )
+    for a, b in line:
+        pl.semaphore_signal(
+            barrier, inc=1, device_id=(y, zs[0] + (xs[a] + cs[b])), device_id_type=MESH
+        )
+
     label = labels[...]
     owner = label >> 1
     dy, dz = ((owner >> 5) - y) & 3, ((owner >> 3) - z) & 3
@@ -86,7 +91,21 @@
     )
     meta_send[...] = meta.astype(I32).reshape(N, 1, N)
 
-    pl.semaphore_wait(barrier, N - 1)
+    def pack(chunk):
+        slot = lax.broadcasted_iota(I32, (CH, ROWS), 0) + chunk * CH
+        chosen = (slot == target).astype(BF16)
+        packed = jnp.dot(chosen, emb[...], preferred_element_type=F32)
+        send[chunk * CH : (chunk + 1) * CH, :] = packed.astype(BF16)
+
+    fetch.wait()
+    pack(0)
+    pl.semaphore_wait(barrier, len(plane) + len(line))
+    for a, b in line:
+        pl.semaphore_signal(
+            planes_sem, inc=1, device_id=(y, zs[0] + (xs[a] + cs[b])), device_id_type=MESH
+        )
+    pack(1)
+    pl.semaphore_wait(planes_sem, len(line))
 
     def send_one(k, carry):
         device = partner(k, 1)
@@ -103,15 +122,10 @@
         ).start()
         return carry
 
-    def pack(chunk, carry):
-        slot = lax.broadcasted_iota(I32, (CH, ROWS), 0) + chunk * CH
-        chosen = (slot == target).astype(BF16)
-        packed = jnp.dot(chosen, emb[...], preferred_element_type=F32)
-        send[at(chunk * CH, CH), :] = packed.astype(BF16)
-        lax.fori_loop(jnp.maximum(chunk * PER, 1), (chunk + 1) * PER, send_one, 0)
-        return carry
-
-    lax.fori_loop(0, NCH, pack, 0)
+    for chunk in range(NCH):
+        lax.fori_loop(max(chunk * PER, 1), (chunk + 1) * PER, send_one, 0)
+        if 1 <= chunk < NCH - 1:
+            pack(chunk + 1)
 
     column = jnp.broadcast_to(target, (N, ROWS)).T
     lanes = lax.broadcasted_iota(I32, (ROWS, N), 1)
@@ -126,14 +140,23 @@
     )
     spread = jnp.ones((N, N), BF16)
 
-    def weights(a, b):
-        score = lax.dot_general(
-            left[at(a * CH, CH), :], right[at(b * CH, CH), :],
-            (((1,), (1,)), ((), ())), preferred_element_type=F32,
-        )
-        return jnp.exp2(score * SCALE)
-
-    for chunk in range(NCH):
+    def block(start, size, cols):
+        parts = []
+        for col in cols:
+            score = lax.dot_general(
+                left[start : start + size, :], right[col * CH : (col + 1) * CH, :],
+                (((1,), (1,)), ((), ())), preferred_element_type=F32,
+            )
+            weight = jnp.exp(score * 40.0)
+            if start == col * CH:
+                weight = jnp.where(diagonal, 0.0, weight)
+            parts.append(weight.astype(BF16))
+        weight = parts[0] if len(parts) == 1 else jnp.concatenate(parts, axis=1)
+        return jnp.dot(
+            weight, rows[cols[0] * CH : (cols[-1] + 1) * CH, :], preferred_element_type=F32
+        )
+
+    def arrive(chunk):
         first = 1 if chunk == 0 else 0
         base, count = chunk * CH + first * SLOT, CH - first * SLOT
         here = slice(chunk * CH, (chunk + 1) * CH)
@@ -163,25 +186,14 @@
         left[here, E:] = ((lane < 3) & (lane != kind)).astype(BF16)
         right[here, E:] = jnp.where(lane == kind, -APART, 0.0).astype(BF16)
 
-        own = jnp.where(diagonal, 0.0, weights(chunk, chunk)).astype(BF16)
-        total[here, :] = jnp.dot(own, rows[here, :], preferred_element_type=F32)
-
-        def earlier(b, carry, chunk=chunk, here=here):
-            there = at(b * CH, CH)
-            weight = weights(chunk, b).astype(BF16)
-            total[here, :] += jnp.dot(weight, rows[there, :], preferred_element_type=F32)
-            return carry
-
-        lax.fori_loop(0, chunk, earlier, 0)
-
-        def later(b, carry, chunk=chunk, here=here):
-            there = at(b * CH, CH)
-            weight = weights(b, chunk).astype(BF16)
-            total[there, :] += jnp.dot(weight, rows[here, :], preferred_element_type=F32)
-            return carry
-
-        if chunk < NCH - 1:
-            lax.fori_loop(0, chunk, later, 0)
+    for chunk in range(NCH - 1):
+        arrive(chunk)
+        here = slice(chunk * CH, (chunk + 1) * CH)
+        total[here, :] = block(chunk * CH, CH, range(chunk + 1))
+        for start in range(0, chunk * CH, 2 * CH):
+            size = min(2 * CH, chunk * CH - start)
+            total[start : start + size, :] += block(start, size, range(chunk, chunk + 1))
+    arrive(NCH - 1)
 
     def return_one(k, carry):
         pltpu.make_async_remote_copy(
@@ -191,26 +203,18 @@
         ).start()
         return carry
 
-    def finish(b, carry):
-        there = at(b * CH, CH)
-        full = total[there, :]
-
-        def last(full):
-            weight = weights(b, NCH - 1).astype(BF16)
-            return full + jnp.dot(
-                weight, rows[(NCH - 1) * CH :, :], preferred_element_type=F32
-            )
-
-        full = lax.cond(b < NCH - 1, last, lambda full: full, full)
+    for chunk in range(NCH):
+        here = slice(chunk * CH, (chunk + 1) * CH)
+        if chunk < NCH - 1:
+            full = total[here, :] + block(chunk * CH, CH, range(NCH - 1, NCH))
+        else:
+            full = block(chunk * CH, CH, range(NCH))
         inverse = 1.0 / (1.0 + full[:, E:])
         for part in range(E // N):
             span = slice(part * N, (part + 1) * N)
-            mixed = recv[there, span].astype(F32) - full[:, span] * inverse
-            result[there, span] = mixed.astype(BF16)
-        lax.fori_loop(jnp.maximum(b * PER, 1), (b + 1) * PER, return_one, 0)
-        return carry
-
-    lax.fori_loop(0, NCH, finish, 0)
+            mixed = rows[here, span].astype(F32) - full[:, span] * inverse
+            result[here, span] = mixed.astype(BF16)
+        lax.fori_loop(max(chunk * PER, 1), (chunk + 1) * PER, return_one, 0)
     returned[0:SLOT, :] = result[0:SLOT, :]
 
     for chunk in range(NCH):
@@ -237,9 +241,13 @@
     return pl.pallas_call(
         kernel,
         out_shape=jax.ShapeDtypeStruct((ROWS, E), BF16),
-        in_specs=[pl.BlockSpec(memory_space=pltpu.VMEM)] * 2,
+        in_specs=[
+            pl.BlockSpec(memory_space=pl.ANY),
+            pl.BlockSpec(memory_space=pltpu.VMEM),
+        ],
         out_specs=pl.BlockSpec(memory_space=pltpu.VMEM),
         scratch_shapes=[
+            pltpu.VMEM((ROWS, E), BF16),
             pltpu.VMEM((SLOTS, E), BF16),
             pltpu.VMEM((N, 1, N), I32),
             pltpu.VMEM((SLOTS, E), BF16),
@@ -251,6 +259,8 @@
             pltpu.VMEM((SLOTS, E), BF16),
             pltpu.VMEM((SLOTS, E), BF16),
             pltpu.VMEM((ROWS, SLOTS), BF16),
+            pltpu.SemaphoreType.DMA,
+            pltpu.SemaphoreType.REGULAR,
             pltpu.SemaphoreType.DMA,
             pltpu.SemaphoreType.DMA,
             pltpu.SemaphoreType.DMA,

time: 82.9 us -> 58.9 us (0.71)
  Pallas kernels: 80.6 us -> 56.6 us
    pallas_call x1, Pallas kernels: 80.6 us -> 56.6 us  [on_device(): pl.pallas_call(kernel, out_shape=jax.ShapeDtypeStruct((ROWS, E), BF16), i...]
where the time goes in v2:
time: 58.9 us; the launch traced here: 58.7 us
  Pallas kernels  56.6 us (96%)
  local copies, waits for them, and re-layouts  2.09 us (4%)
    pallas_call x1, Pallas kernels, on_device(): pl.pallas_call(kernel, out_shape=jax.ShapeDtypeStruct((ROWS, E), BF16), i...  56.6 us
    unnamed x1, local copies, waits for them, and re-layouts  2.09 us

profile of v2, /device:TPU:1, one launch (start us, length us, event | category | flops | bytes accessed | tf_op | source)
XLA Modules:
  0.0 58.7 jit_solution(10171227074835537571)
XLA Ops:
  0.0 56.6 %shard_map.28 = bf16[1024,384]{1,0:T(8,128)(2,1)} custom-call(bf16[1024,384]{1,0:T(8,128)(2,1)} %emb_hbm.1, s32[1,1024]{1,0:T(1,128)} %bitcast.1), custom_call_target="tpu_custom_call" | custom-call | tf_op jit(solution)/shard_map/pallas_call | solution.py:241
  56.6 2.1 %copy.4 = bf16[1024,384]{1,0:T(8,128)(2,1)} copy(bf16[1024,384]{1,0:T(8,128)(2,1)} %shard_map.28) | data formatting | bytes 1572864

commit v3 on v2

--- a/solution.py
+++ b/solution.py
@@ -15,61 +15,59 @@
 CH = 256
 NCH = SLOTS // CH
 PER = CH // SLOT
-STEP, BACK = 91, 83
+NEAR = 23
+EARLY = 4
 APART = 16.0
 
 
-def rank_of(shift):
-    return (shift * BACK) & (N - 1)
-
-
-def coords():
-    tm, cl = lax.axis_index("tm"), lax.axis_index("clus")
-    return tm, cl // 8, (cl // 2) % 4, cl % 2
-
-
-def partner(k, sign):
-    shift = lax.rem(k * STEP, N)
-    dy, dz, dx = lax.div(shift, 32), lax.rem(lax.div(shift, 8), 4), lax.rem(lax.div(shift, 2), 4)
-    y, z, x, c = coords()
-    if sign < 0:
-        dy, dz, dx = 4 - dy, 4 - dz, 4 - dx
-    y, z, x, c = lax.rem(y + dy, 4), lax.rem(z + dz, 4), lax.rem(x + dx, 4), lax.rem(c + shift, 2)
-    return (y, z * 8 + x * 2 + c)
-
-
-def at(start, size):
-    return pl.ds(pl.multiple_of(start, 16), size)
+def shift_of(k):
+    if k < NEAR:
+        turn, mate = (0, k // 3) if k % 3 == 0 else (k - k // 3, 0)
+    else:
+        turn, mate = (k - 16) // 7, (k - 16) % 7 + 1
+    place = turn * 7 % 16
+    return place // 4, place % 4, mate // 2, mate % 2
+
+
+def order_of(dy, dz, dx, dc):
+    turn, mate = ((dy * 4 + dz) * 7) & 15, dx * 2 + dc
+    near = jnp.where(mate == 0, turn + (jnp.maximum(turn - 1, 0) >> 1), 3 * mate)
+    return jnp.where((mate == 0) | (turn == 0), near, 15 + 7 * turn + mate)
 
 
 def kernel(
-    emb_hbm, labels, out,
-    emb, send, meta_send, recv, meta_recv, rows, left, right, total, result, returned, pick,
-    fetch_sem, planes_sem, send_sem, meta_send_sem, back_sem, recv_sem, meta_sem, return_sem,
+    emb_hbm, labels_hbm, out,
+    emb, labels, send, meta_send, recv, meta_recv, rows, left, right, total, result, returned, pick,
+    fetch_sem, labels_sem, planes_sem,
+    send_sem, meta_send_sem, back_sem, recv_sem, meta_sem, return_sem,
 ):
+    fetch_labels = pltpu.make_async_copy(labels_hbm, labels, labels_sem)
+    fetch_labels.start()
     fetch = pltpu.make_async_copy(emb_hbm, emb, fetch_sem)
     fetch.start()
 
-    y, z, x, c = coords()
-    barrier = pltpu.get_barrier_semaphore()
-    plane = [(a, b) for a in range(4) for b in range(4) if (a, b) != (0, 0)]
-    line = [(a, b) for a in range(4) for b in range(2) if (a, b) != (0, 0)]
+    tm, cl = lax.axis_index("tm"), lax.axis_index("clus")
+    y, z, x, c = tm, cl // 8, (cl // 2) % 4, cl % 2
     ys, zs = [lax.rem(y + d, 4) for d in range(4)], [lax.rem(z + d, 4) * 8 for d in range(4)]
     xs, cs = [lax.rem(x + d, 4) * 2 for d in range(4)], [c, 1 - c]
-    for a, b in plane:
-        pl.semaphore_signal(
-            barrier, inc=1, device_id=(ys[a], zs[b] + (xs[0] + c)), device_id_type=MESH
-        )
-    for a, b in line:
-        pl.semaphore_signal(
-            barrier, inc=1, device_id=(y, zs[0] + (xs[a] + cs[b])), device_id_type=MESH
-        )
-
+    barrier = pltpu.get_barrier_semaphore()
+
+    def partner(k, sign):
+        dy, dz, dx, dc = shift_of(k)
+        return (ys[sign * dy % 4], zs[sign * dz % 4] + (xs[sign * dx % 4] + cs[dc]))
+
+    def tell(sem, k):
+        pl.semaphore_signal(sem, inc=1, device_id=partner(k, 1), device_id_type=MESH)
+
+    for k in range(1, NEAR):
+        tell(barrier, k)
+
+    fetch_labels.wait()
     label = labels[...]
     owner = label >> 1
     dy, dz = ((owner >> 5) - y) & 3, ((owner >> 3) - z) & 3
     dx, dc = ((owner >> 1) - x) & 3, (owner - c) & 1
-    order = rank_of(dy * 32 + dz * 8 + dx * 2 + dc)
+    order = order_of(dy, dz, dx, dc)
     hits = (order == lax.broadcasted_iota(I32, (N, ROWS), 0)).astype(F32)
     upper = (
         lax.broadcasted_iota(I32, (CH, CH), 0) <= lax.broadcasted_iota(I32, (CH, CH), 1)
@@ -97,35 +95,31 @@
         packed = jnp.dot(chosen, emb[...], preferred_element_type=F32)
         send[chunk * CH : (chunk + 1) * CH, :] = packed.astype(BF16)
 
-    fetch.wait()
-    pack(0)
-    pl.semaphore_wait(barrier, len(plane) + len(line))
-    for a, b in line:
-        pl.semaphore_signal(
-            planes_sem, inc=1, device_id=(y, zs[0] + (xs[a] + cs[b])), device_id_type=MESH
-        )
-    pack(1)
-    pl.semaphore_wait(planes_sem, len(line))
-
-    def send_one(k, carry):
-        device = partner(k, 1)
-        chunk = k // PER
+    def send_one(k):
+        device, chunk, here = partner(k, 1), k // PER, slice(k * SLOT, (k + 1) * SLOT)
         pltpu.make_async_remote_copy(
             src_ref=meta_send.at[k], dst_ref=meta_recv.at[k],
             send_sem=meta_send_sem, recv_sem=meta_sem.at[chunk],
             device_id=device, device_id_type=MESH,
         ).start()
         pltpu.make_async_remote_copy(
-            src_ref=send.at[at(k * SLOT, SLOT)], dst_ref=recv.at[at(k * SLOT, SLOT)],
+            src_ref=send.at[here], dst_ref=recv.at[here],
             send_sem=send_sem, recv_sem=recv_sem.at[chunk],
             device_id=device, device_id_type=MESH,
         ).start()
-        return carry
-
+
+    fetch.wait()
+    pack(0)
+    pl.semaphore_wait(barrier, NEAR - 1)
+    for k in range(3, NEAR, 3):
+        tell(planes_sem, k)
     for chunk in range(NCH):
-        lax.fori_loop(max(chunk * PER, 1), (chunk + 1) * PER, send_one, 0)
-        if 1 <= chunk < NCH - 1:
-            pack(chunk + 1)
+        if chunk > 0:
+            pack(chunk)
+        for k in range(max(chunk * PER, 1), (chunk + 1) * PER):
+            if k == NEAR:
+                pl.semaphore_wait(planes_sem, NEAR // 3)
+            send_one(k)
 
     column = jnp.broadcast_to(target, (N, ROWS)).T
     lanes = lax.broadcasted_iota(I32, (ROWS, N), 1)
@@ -188,24 +182,26 @@
 
     for chunk in range(NCH - 1):
         arrive(chunk)
-        here = slice(chunk * CH, (chunk + 1) * CH)
-        total[here, :] = block(chunk * CH, CH, range(chunk + 1))
-        for start in range(0, chunk * CH, 2 * CH):
-            size = min(2 * CH, chunk * CH - start)
+        if chunk < EARLY:
+            here = slice(chunk * CH, (chunk + 1) * CH)
+            total[here, :] = block(chunk * CH, CH, range(chunk + 1))
+        done = min(chunk, EARLY) * CH
+        for start in range(0, done, 2 * CH):
+            size = min(2 * CH, done - start)
             total[start : start + size, :] += block(start, size, range(chunk, chunk + 1))
     arrive(NCH - 1)
 
-    def return_one(k, carry):
+    def return_one(k):
+        here = slice(k * SLOT, (k + 1) * SLOT)
         pltpu.make_async_remote_copy(
-            src_ref=result.at[at(k * SLOT, SLOT)], dst_ref=returned.at[at(k * SLOT, SLOT)],
+            src_ref=result.at[here], dst_ref=returned.at[here],
             send_sem=back_sem, recv_sem=return_sem.at[k // PER],
             device_id=partner(k, -1), device_id_type=MESH,
         ).start()
-        return carry
 
     for chunk in range(NCH):
         here = slice(chunk * CH, (chunk + 1) * CH)
-        if chunk < NCH - 1:
+        if chunk < EARLY:
             full = total[here, :] + block(chunk * CH, CH, range(NCH - 1, NCH))
         else:
             full = block(chunk * CH, CH, range(NCH))
@@ -214,7 +210,8 @@
             span = slice(part * N, (part + 1) * N)
             mixed = rows[here, span].astype(F32) - full[:, span] * inverse
             result[here, span] = mixed.astype(BF16)
-        lax.fori_loop(max(chunk * PER, 1), (chunk + 1) * PER, return_one, 0)
+        for k in range(max(chunk * PER, 1), (chunk + 1) * PER):
+            return_one(k)
     returned[0:SLOT, :] = result[0:SLOT, :]
 
     for chunk in range(NCH):
@@ -237,17 +234,21 @@
     pltpu.make_async_copy(result.at[sent], result.at[sent], back_sem).wait()
 
 
+def deliver(held, out, sem):
+    copy = pltpu.make_async_copy(held, out, sem)
+    copy.start()
+    copy.wait()
+
+
 def on_device(embedding, cluster_of):
-    return pl.pallas_call(
+    held = pl.pallas_call(
         kernel,
-        out_shape=jax.ShapeDtypeStruct((ROWS, E), BF16),
-        in_specs=[
-            pl.BlockSpec(memory_space=pl.ANY),
-            pl.BlockSpec(memory_space=pltpu.VMEM),
-        ],
+        out_shape=pltpu.VMEM((ROWS, E), BF16),
+        in_specs=[pl.BlockSpec(memory_space=pltpu.HBM)] * 2,
         out_specs=pl.BlockSpec(memory_space=pltpu.VMEM),
         scratch_shapes=[
             pltpu.VMEM((ROWS, E), BF16),
+            pltpu.VMEM((1, ROWS), I32),
             pltpu.VMEM((SLOTS, E), BF16),
             pltpu.VMEM((N, 1, N), I32),
             pltpu.VMEM((SLOTS, E), BF16),
@@ -255,10 +256,11 @@
             pltpu.VMEM((SLOTS, E + N), BF16),
             pltpu.VMEM((SLOTS, E + N), BF16),
             pltpu.VMEM((SLOTS, E + N), BF16),
-            pltpu.VMEM((SLOTS, E + N), F32),
+            pltpu.VMEM((EARLY * CH, E + N), F32),
             pltpu.VMEM((SLOTS, E), BF16),
             pltpu.VMEM((SLOTS, E), BF16),
             pltpu.VMEM((ROWS, SLOTS), BF16),
+            pltpu.SemaphoreType.DMA,
             pltpu.SemaphoreType.DMA,
             pltpu.SemaphoreType.REGULAR,
             pltpu.SemaphoreType.DMA,
@@ -272,6 +274,13 @@
             collective_id=0, has_side_effects=True, vmem_limit_bytes=56 << 20
         ),
     )(embedding, cluster_of.reshape(1, ROWS))
+    return pl.pallas_call(
+        deliver,
+        out_shape=jax.ShapeDtypeStruct((ROWS, E), BF16),
+        in_specs=[pl.BlockSpec(memory_space=pltpu.VMEM)],
+        out_specs=pl.BlockSpec(memory_space=pl.ANY),
+        scratch_shapes=[pltpu.SemaphoreType.DMA],
+    )(held)
 
 
 def solution(mesh):

time: 58.9 us -> 57.4 us (0.975)
  local copies, waits for them, and re-layouts: 2.09 us -> 0.88 us
    unnamed x1 -> x2, local copies, waits for them, and re-layouts: 2.09 us -> 0.88 us
    pallas_call x1 -> x2, Pallas kernels: 56.6 us -> 56.2 us  [the longest x1 54.2 us: on_device(): pl.pallas_call(kernel, out_shape=pltpu.VMEM((ROWS, E), BF16), in_specs=[p...]
where the time goes in v3:
time: 57.4 us; the launch traced here: 57.2 us
  Pallas kernels  56.2 us (98%)
  local copies, waits for them, and re-layouts  0.88 us (2%)
    pallas_call x1, Pallas kernels, on_device(): pl.pallas_call(kernel, out_shape=pltpu.VMEM((ROWS, E), BF16), in_specs=[p...  54.2 us
    pallas_call x1, Pallas kernels, on_device(): pl.pallas_call(deliver, out_shape=jax.ShapeDtypeStruct((ROWS, E), BF16),...  2.02 us

profile of v3, /device:TPU:1, one launch (start us, length us, event | category | flops | bytes accessed | tf_op | source)
XLA Modules:
  0.0 57.2 jit_solution(11320261456814038441)
XLA Ops:
  0.0 54.2 %shard_map.28.held = bf16[1024,384]{1,0:T(8,128)(2,1)S(1)} custom-call(bf16[1024,384]{1,0:T(8,128)(2,1)} %emb_hbm.1, s32[1,1024]{1,0:T(1,128)} %bitcast.1), custom_call_target="tpu_custom_call" | custom-call | tf_op jit(solution)/shard_map/pallas_call | solution.py:244
  54.2 0.0 copy-start
  54.2 0.9 %copy-done = bf16[1024,384]{1,0:T(8,128)(2,1)} copy-done((bf16[1024,384]{1,0:T(8,128)(2,1)}, bf16[1024,384]{1,0:T(8,128)(2,1)S(1)}, u32[]{:S(2)}) %copy-start) | copy-done | bytes 786456
  55.1 2.0 %shard_map.29 = bf16[1024,384]{1,0:T(8,128)(2,1)} custom-call(bf16[1024,384]{1,0:T(8,128)(2,1)} %copy-done), custom_call_target="tpu_custom_call" | custom-call | tf_op jit(solution)/shard_map/pallas_call | solution.py:277
Async XLA Ops:
  54.2 0.9 %copy-start = (bf16[1024,384]{1,0:T(8,128)(2,1)}, bf16[1024,384]{1,0:T(8,128)(2,1)S(1)}, u32[]{:S(2)}) copy-start(bf16[1024,384]{1,0:T(8,128)(2,1)S(1)} %shard_map.28.held) | copy-start | bytes 2359300

commit v4 on v3

--- a/solution.py
+++ b/solution.py
@@ -16,23 +16,27 @@
 NCH = SLOTS // CH
 PER = CH // SLOT
 NEAR = 23
-EARLY = 4
+EARLY = range(1, 5)
+BACK = tuple((i * CH, (i + 1) * CH) for i in range(2, NCH)) + ((CH, 2 * CH), (0, CH))
 APART = 16.0
 
 
-def shift_of(k):
-    if k < NEAR:
-        turn, mate = (0, k // 3) if k % 3 == 0 else (k - k // 3, 0)
-    else:
-        turn, mate = (k - 16) // 7, (k - 16) % 7 + 1
-    place = turn * 7 % 16
-    return place // 4, place % 4, mate // 2, mate % 2
-
-
-def order_of(dy, dz, dx, dc):
-    turn, mate = ((dy * 4 + dz) * 7) & 15, dx * 2 + dc
-    near = jnp.where(mate == 0, turn + (jnp.maximum(turn - 1, 0) >> 1), 3 * mate)
-    return jnp.where((mate == 0) | (turn == 0), near, 15 + 7 * turn + mate)
+def key_of(dy, dz, dx, dc):
+    place, mate = dy * 4 + dz, dx * 2 + dc
+    hops = sum(jnp.minimum(d, 4 - d) if isinstance(d, jax.Array) else min(d, 4 - d) for d in (dy, dz, dx))
+    mixed = ((place * 8 + mate) * 83) % N
+    near = (place * mate == 0) * 1
+    return (1 - near) * (1 + (hops < 3)) * N + mixed
+
+
+SHIFTS = sorted(
+    ((dy, dz, dx, dc) for dy in range(4) for dz in range(4) for dx in range(4) for dc in range(2)),
+    key=lambda shift: key_of(*shift),
+)
+
+
+def near_line(k):
+    return SHIFTS[k][0] == SHIFTS[k][1] == 0
 
 
 def kernel(
@@ -53,7 +57,7 @@
     barrier = pltpu.get_barrier_semaphore()
 
     def partner(k, sign):
-        dy, dz, dx, dc = shift_of(k)
+        dy, dz, dx, dc = SHIFTS[k]
         return (ys[sign * dy % 4], zs[sign * dz % 4] + (xs[sign * dx % 4] + cs[dc]))
 
     def tell(sem, k):
@@ -67,7 +71,10 @@
     owner = label >> 1
     dy, dz = ((owner >> 5) - y) & 3, ((owner >> 3) - z) & 3
     dx, dc = ((owner >> 1) - x) & 3, (owner - c) & 1
-    order = order_of(dy, dz, dx, dc)
+    shift = lax.broadcasted_iota(I32, (N, 1), 0)
+    keys = key_of(shift >> 5, (shift >> 3) & 3, (shift >> 1) & 3, shift & 1)
+    ahead = (keys < key_of(dy, dz, dx, dc)).astype(F32)
+    order = jnp.sum(ahead, axis=0, keepdims=True).astype(I32)
     hits = (order == lax.broadcasted_iota(I32, (N, ROWS), 0)).astype(F32)
     upper = (
         lax.broadcasted_iota(I32, (CH, CH), 0) <= lax.broadcasted_iota(I32, (CH, CH), 1)
@@ -111,14 +118,15 @@
     fetch.wait()
     pack(0)
     pl.semaphore_wait(barrier, NEAR - 1)
-    for k in range(3, NEAR, 3):
+    line = [k for k in range(1, NEAR) if near_line(k)]
+    for k in line:
         tell(planes_sem, k)
     for chunk in range(NCH):
         if chunk > 0:
             pack(chunk)
         for k in range(max(chunk * PER, 1), (chunk + 1) * PER):
             if k == NEAR:
-                pl.semaphore_wait(planes_sem, NEAR // 3)
+                pl.semaphore_wait(planes_sem, len(line))
             send_one(k)
 
     column = jnp.broadcast_to(target, (N, ROWS)).T
@@ -182,51 +190,59 @@
 
     for chunk in range(NCH - 1):
         arrive(chunk)
-        if chunk < EARLY:
-            here = slice(chunk * CH, (chunk + 1) * CH)
+        if chunk in EARLY:
+            here = slice((chunk - EARLY[0]) * CH, (chunk - EARLY[0] + 1) * CH)
             total[here, :] = block(chunk * CH, CH, range(chunk + 1))
-        done = min(chunk, EARLY) * CH
+        done = max(min(chunk, EARLY[-1] + 1) - EARLY[0], 0) * CH
         for start in range(0, done, 2 * CH):
             size = min(2 * CH, done - start)
-            total[start : start + size, :] += block(start, size, range(chunk, chunk + 1))
+            total[start : start + size, :] += block(
+                start + EARLY[0] * CH, size, range(chunk, chunk + 1)
+            )
     arrive(NCH - 1)
 
     def return_one(k):
         here = slice(k * SLOT, (k + 1) * SLOT)
         pltpu.make_async_remote_copy(
             src_ref=result.at[here], dst_ref=returned.at[here],
-            send_sem=back_sem, recv_sem=return_sem.at[k // PER],
+            send_sem=back_sem, recv_sem=return_sem.at[[k * SLOT in range(*part) for part in BACK].index(True)],
             device_id=partner(k, -1), device_id_type=MESH,
         ).start()
 
-    for chunk in range(NCH):
-        here = slice(chunk * CH, (chunk + 1) * CH)
-        if chunk < EARLY:
-            full = total[here, :] + block(chunk * CH, CH, range(NCH - 1, NCH))
+    def finish(start, size):
+        here = slice(start, start + size)
+        if start // CH in EARLY:
+            there = slice(start - EARLY[0] * CH, start - EARLY[0] * CH + size)
+            full = total[there, :] + block(start, size, range(NCH - 1, NCH))
         else:
-            full = block(chunk * CH, CH, range(NCH))
+            full = block(start, size, range(NCH))
         inverse = 1.0 / (1.0 + full[:, E:])
         for part in range(E // N):
             span = slice(part * N, (part + 1) * N)
             mixed = rows[here, span].astype(F32) - full[:, span] * inverse
             result[here, span] = mixed.astype(BF16)
-        for k in range(max(chunk * PER, 1), (chunk + 1) * PER):
+        for k in range(max(start // SLOT, NEAR), (start + size) // SLOT):
             return_one(k)
+
+    finish(CH, N)
+    finish(CH + N, N)
+    for start in range(2 * CH, SLOTS, CH):
+        finish(start, CH)
+    finish(0, CH)
+    for k in range(1, NEAR):
+        return_one(k)
     returned[0:SLOT, :] = result[0:SLOT, :]
 
-    for chunk in range(NCH):
-        first = 1 if chunk == 0 else 0
-        base, count = chunk * CH + first * SLOT, CH - first * SLOT
-        here = slice(chunk * CH, (chunk + 1) * CH)
+    for index, (begin, end) in enumerate(BACK):
+        base = max(begin, SLOT)
         pltpu.make_async_copy(
-            returned.at[base : base + count], returned.at[base : base + count],
-            return_sem.at[chunk],
+            returned.at[base:end], returned.at[base:end], return_sem.at[index]
         ).wait()
-        part = jnp.dot(pick[:, here], returned[here, :], preferred_element_type=F32).astype(BF16)
-        if chunk == 0:
-            out[...] = part
+        part = jnp.dot(pick[:, begin:end], returned[begin:end, :], preferred_element_type=F32)
+        if index == 0:
+            out[...] = part.astype(BF16)
         else:
-            out[...] += part
+            out[...] += part.astype(BF16)
 
     sent = slice(SLOT, SLOTS)
     pltpu.make_async_copy(send.at[sent], send.at[sent], send_sem).wait()
@@ -256,7 +272,7 @@
             pltpu.VMEM((SLOTS, E + N), BF16),
             pltpu.VMEM((SLOTS, E + N), BF16),
             pltpu.VMEM((SLOTS, E + N), BF16),
-            pltpu.VMEM((EARLY * CH, E + N), F32),
+            pltpu.VMEM((len(EARLY) * CH, E + N), F32),
             pltpu.VMEM((SLOTS, E), BF16),
             pltpu.VMEM((SLOTS, E), BF16),
             pltpu.VMEM((ROWS, SLOTS), BF16),
@@ -268,7 +284,7 @@
             pltpu.SemaphoreType.DMA,
             pltpu.SemaphoreType.DMA((NCH,)),
             pltpu.SemaphoreType.DMA((NCH,)),
-            pltpu.SemaphoreType.DMA((NCH,)),
+            pltpu.SemaphoreType.DMA((len(BACK),)),
         ],
         compiler_params=pltpu.CompilerParams(
             collective_id=0, has_side_effects=True, vmem_limit_bytes=56 << 20
@@ -280,6 +296,7 @@
         in_specs=[pl.BlockSpec(memory_space=pltpu.VMEM)],
         out_specs=pl.BlockSpec(memory_space=pl.ANY),
         scratch_shapes=[pltpu.SemaphoreType.DMA],
+        compiler_params=pltpu.CompilerParams(vmem_limit_bytes=2 << 20),
     )(held)
 
 

time: 57.4 us -> 55.2 us (0.962)
  Pallas kernels: 56.2 us -> 54.9 us
  local copies, waits for them, and re-layouts: 0.88 us -> 0 us
    pallas_call x1, Pallas kernels: 2.02 us -> 0.89 us  [on_device(): pl.pallas_call(deliver, out_shape=jax.ShapeDtypeStruct((ROWS, E), BF16),...]
    unnamed x2 -> x0, local copies, waits for them, and re-layouts: 0.88 us -> none
where the time goes in v4:
time: 55.2 us; the launch traced here: 55.1 us
  Pallas kernels  54.9 us (99%)
    pallas_call x1, Pallas kernels, on_device(): pl.pallas_call(kernel, out_shape=pltpu.VMEM((ROWS, E), BF16), in_specs=[p...  54 us

profile of v4, /device:TPU:1, one launch (start us, length us, event | category | flops | bytes accessed | tf_op | source)
XLA Modules:
  0.0 55.1 jit_solution(18019664947968285153)
XLA Ops:
  0.0 54.0 %shard_map.28.held = bf16[1024,384]{1,0:T(8,128)(2,1)S(1)} custom-call(bf16[1024,384]{1,0:T(8,128)(2,1)} %emb_hbm.1, s32[1,1024]{1,0:T(1,128)} %bitcast.1), custom_call_target="tpu_custom_call" | custom-call | tf_op jit(solution)/shard_map/pallas_call | solution.py:260
  54.0 0.9 %shard_map.29 = bf16[1024,384]{1,0:T(8,128)(2,1)} custom-call(bf16[1024,384]{1,0:T(8,128)(2,1)S(1)} %shard_map.28.held), custom_call_target="tpu_custom_call" | custom-call | tf_op jit(solution)/shard_map/pallas_call | solution.py:293

commit v5 on v4

--- a/solution.py
+++ b/solution.py
@@ -16,8 +16,8 @@
 NCH = SLOTS // CH
 PER = CH // SLOT
 NEAR = 23
-EARLY = range(1, 5)
-BACK = tuple((i * CH, (i + 1) * CH) for i in range(2, NCH)) + ((CH, 2 * CH), (0, CH))
+EARLY = range(1, 3)
+BACK = tuple((i * CH, (i + 1) * CH) for i in range(2, NCH)) + ((0, 2 * CH),)
 APART = 16.0
 
 
@@ -224,10 +224,10 @@
         for k in range(max(start // SLOT, NEAR), (start + size) // SLOT):
             return_one(k)
 
-    finish(CH, N)
     finish(CH + N, N)
     for start in range(2 * CH, SLOTS, CH):
         finish(start, CH)
+    finish(CH, N)
     finish(0, CH)
     for k in range(1, NEAR):
         return_one(k)

time: 55.2 us -> 54.4 us (0.986)
  Pallas kernels: 54.9 us -> 54.1 us
    pallas_call x1, Pallas kernels: 54 us -> 53.2 us  [on_device(): pl.pallas_call(kernel, out_shape=pltpu.VMEM((ROWS, E), BF16), in_specs=[p...]
where the time goes in v5:
time: 54.4 us; the launch traced here: 54.3 us
  Pallas kernels  54.1 us (99%)
    pallas_call x1, Pallas kernels, on_device(): pl.pallas_call(kernel, out_shape=pltpu.VMEM((ROWS, E), BF16), in_specs=[p...  53.2 us

profile of v5, /device:TPU:1, one launch (start us, length us, event | category | flops | bytes accessed | tf_op | source)
XLA Modules:
  0.0 54.3 jit_solution(8974871905750340179)
XLA Ops:
  0.0 53.2 %shard_map.28.held = bf16[1024,384]{1,0:T(8,128)(2,1)S(1)} custom-call(bf16[1024,384]{1,0:T(8,128)(2,1)} %emb_hbm.1, s32[1,1024]{1,0:T(1,128)} %bitcast.1), custom_call_target="tpu_custom_call" | custom-call | tf_op jit(solution)/shard_map/pallas_call | solution.py:260
  53.2 0.9 %shard_map.29 = bf16[1024,384]{1,0:T(8,128)(2,1)} custom-call(bf16[1024,384]{1,0:T(8,128)(2,1)S(1)} %shard_map.28.held), custom_call_target="tpu_custom_call" | custom-call | tf_op jit(solution)/shard_map/pallas_call | solution.py:293

commit v6 on v5

--- a/solution.py
+++ b/solution.py
@@ -24,7 +24,7 @@
 def key_of(dy, dz, dx, dc):
     place, mate = dy * 4 + dz, dx * 2 + dc
     hops = sum(jnp.minimum(d, 4 - d) if isinstance(d, jax.Array) else min(d, 4 - d) for d in (dy, dz, dx))
-    mixed = ((place * 8 + mate) * 83) % N
+    mixed = ((place * 8 + mate) * 117) % N
     near = (place * mate == 0) * 1
     return (1 - near) * (1 + (hops < 3)) * N + mixed
 

time: 54.4 us -> 53.8 us (0.989)
    pallas_call x1, Pallas kernels: 53.2 us -> 52.7 us  [on_device(): pl.pallas_call(kernel, out_shape=pltpu.VMEM((ROWS, E), BF16), in_specs=[p...]
where the time goes in v6:
time: 53.8 us; the launch traced here: 53.7 us
  Pallas kernels  53.6 us (100%)
    pallas_call x1, Pallas kernels, on_device(): pl.pallas_call(kernel, out_shape=pltpu.VMEM((ROWS, E), BF16), in_specs=[p...  52.7 us

profile of v6, /device:TPU:1, one launch (start us, length us, event | category | flops | bytes accessed | tf_op | source)
XLA Modules:
  0.0 53.7 jit_solution(4782531716321185372)
XLA Ops:
  0.0 52.7 %shard_map.28.held = bf16[1024,384]{1,0:T(8,128)(2,1)S(1)} custom-call(bf16[1024,384]{1,0:T(8,128)(2,1)} %emb_hbm.1, s32[1,1024]{1,0:T(1,128)} %bitcast.1), custom_call_target="tpu_custom_call" | custom-call | tf_op jit(solution)/shard_map/pallas_call | solution.py:260
  52.7 0.9 %shard_map.29 = bf16[1024,384]{1,0:T(8,128)(2,1)} custom-call(bf16[1024,384]{1,0:T(8,128)(2,1)S(1)} %shard_map.28.held), custom_call_target="tpu_custom_call" | custom-call | tf_op jit(solution)/shard_map/pallas_call | solution.py:293

commit v7 on v6

--- a/solution.py
+++ b/solution.py
@@ -24,7 +24,7 @@
 def key_of(dy, dz, dx, dc):
     place, mate = dy * 4 + dz, dx * 2 + dc
     hops = sum(jnp.minimum(d, 4 - d) if isinstance(d, jax.Array) else min(d, 4 - d) for d in (dy, dz, dx))
-    mixed = ((place * 8 + mate) * 117) % N
+    mixed = ((place * 8 + mate) * 37) % N
     near = (place * mate == 0) * 1
     return (1 - near) * (1 + (hops < 3)) * N + mixed
 

time: 53.8 us -> 54.1 us (level)
  no operation moved by 1% of the time
where the time goes in v7:
time: 54.1 us; the launch traced here: 54 us
  Pallas kernels  53.8 us (99%)
    pallas_call x1, Pallas kernels, on_device(): pl.pallas_call(kernel, out_shape=pltpu.VMEM((ROWS, E), BF16), in_specs=[p...  52.9 us

profile of v7, /device:TPU:1, one launch (start us, length us, event | category | flops | bytes accessed | tf_op | source)
XLA Modules:
  0.0 54.0 jit_solution(9625989863096935929)
XLA Ops:
  0.0 52.9 %shard_map.28.held = bf16[1024,384]{1,0:T(8,128)(2,1)S(1)} custom-call(bf16[1024,384]{1,0:T(8,128)(2,1)} %emb_hbm.1, s32[1,1024]{1,0:T(1,128)} %bitcast.1), custom_call_target="tpu_custom_call" | custom-call | tf_op jit(solution)/shard_map/pallas_call | solution.py:260
  52.9 0.9 %shard_map.29 = bf16[1024,384]{1,0:T(8,128)(2,1)} custom-call(bf16[1024,384]{1,0:T(8,128)(2,1)S(1)} %shard_map.28.held), custom_call_target="tpu_custom_call" | custom-call | tf_op jit(solution)/shard_map/pallas_call | solution.py:293
